TPU v7x, 32 devices: a whole 2x2x4 slice. The times are simulated.
32 devices in a mesh: groups: 2 (over y), rows: 4 (over z), samp: 2 (over x), sub: 2 (over core).
Axes of the slice: x: 2, y: 2, z: 4, core: 2. Of those that a mesh axis runs over, the one named last changes fastest.
Arguments:
- points: bfloat16 [131072, 256], P(('groups', 'rows', 'samp', 'sub')), parts along dimension 0, may hold values from -6 to 6
- inv_scale: float32 [512], P('groups'), parts along dimension 0, may hold values from 0.6 to 1.8
- labels: int32 [131072, 1], P(('groups', 'rows', 'samp', 'sub')), parts along dimension 0, may hold values from 0 to 3; in each aligned block of 4096 rows (0 to 4095, 4096 to 8191, ...) at most 2048 rows name the same one
- pattern: int32 [4, 1024], P(None, ('groups', 'rows', 'samp', 'sub')), parts along dimension 1, may hold values 0 or 1
- old_bases: bfloat16 [8, 32, 256], P(('groups', 'rows')), parts along dimension 0, may hold values from -0.375 to 0.375
Outputs:
- errors: float32 [4, 131072], P(None, ('groups', 'rows', 'samp', 'sub')), parts along dimension 1
- new_means: float32 [8, 256], P(('groups', 'rows')), parts along dimension 0
- new_bases: float32 [8, 32, 256], P(('groups', 'rows')), parts along dimension 0
There are 2 independent parts, one for each index of `groups`. A program takes and returns all parts, laid end to end along the dimension named above; each array names one. Nothing has to cross between parts.
Inputs may be any that keep to these rules, and one draw needn't show every extreme that they name: `labels`: within the rows of one device no cluster is named more than 2048 times, and some cluster reaches 2048 in some devices; every cluster is named by some point.
All inputs are finite; a program needn't handle non-finite values. No bound on the sum of `pattern` on one device may be relied on, other than what follows from the above.
Results may differ from a plain program's by a relative error of at most 0.0029.
Values may be sent and summed in bfloat16 or wider, within the bound.
A program may use at most 64 MiB of HBM per device.

v0:
```python
import jax
import jax.numpy as jnp
from jax import lax
from jax.sharding import PartitionSpec as P

TILE = 128
STEPS = 2


def arrange(scaled, label_ids, clusters, capacity):
    features = scaled.shape[1]
    member = (label_ids[:, None] == jnp.arange(clusters, dtype=jnp.int32)[None, :]).astype(
        jnp.int32
    )
    ranking = jnp.sum((jnp.cumsum(member, axis=0) - 1) * member, axis=1)
    target = label_ids * capacity + ranking
    buffer = jnp.zeros((clusters * capacity, features), scaled.dtype).at[target].set(scaled)
    return buffer.reshape(clusters, capacity, features)


def refine(subspace, covariance):
    for iteration in range(STEPS):
        mapped = jnp.dot(subspace, covariance, precision=lax.Precision.HIGHEST)
        correlation = jnp.dot(mapped, mapped.T, precision=lax.Precision.HIGHEST)
        factor = jnp.linalg.cholesky(correlation)
        subspace = jax.scipy.linalg.solve_triangular(factor, mapped, lower=True)
    return subspace


def cluster_errors(scaled, row_mask, centers, bases_low):
    clusters, rank_count, features = bases_low.shape
    flat = bases_low.reshape(clusters * rank_count, features)
    shift = jnp.einsum(
        "nrv,nv->nr", bases_low.astype(jnp.float32), centers, precision=lax.Precision.HIGHEST
    )
    center_sq = jnp.sum(centers * centers, axis=1)
    rows_total = scaled.shape[0]
    span = min(1024, rows_total)
    stacked = scaled.reshape(rows_total // span, span, features)

    def one_block(row_block):
        projected = lax.dot_general(
            row_block, flat, (((1,), (1,)), ((), ())), preferred_element_type=jnp.float32
        )
        projected = projected.reshape(span, clusters, rank_count) - shift[None]
        widened = row_block.astype(jnp.float32)
        cross = jnp.dot(widened, centers.T, precision=lax.Precision.HIGHEST)
        distance = jnp.sum(widened * widened, axis=1)[:, None] - 2.0 * cross + center_sq[None, :]
        return (distance - jnp.sum(projected * projected, axis=2)) / features

    result = lax.map(one_block, stacked).reshape(rows_total, clusters)
    return result.T * row_mask


def shards(points, inv_scale, labels, pattern, old_bases):
    clusters = lax.axis_size("rows")
    rows_total, features = points.shape
    capacity = 2 * rows_total // clusters
    owner = lax.axis_index("rows")
    scaled = (points.astype(jnp.float32) * inv_scale[None, :]).astype(jnp.bfloat16)
    label_ids = labels[:, 0]
    member = jnp.arange(clusters, dtype=jnp.int32)[:, None] == label_ids[None, :]
    counts_local = jnp.sum(member.astype(jnp.float32), axis=1)
    sums_local = jnp.dot(member.astype(jnp.bfloat16), scaled, preferred_element_type=jnp.float32)
    counts, totals = lax.psum((counts_local, sums_local), ("rows", "samp", "sub"))
    centers = totals / counts[:, None]
    buffer = arrange(scaled, label_ids, clusters, capacity)
    received = lax.all_to_all(buffer, "rows", split_axis=0, concat_axis=0, tiled=True)
    flat_rows = received.reshape(-1, features)
    partial_value = lax.dot_general(
        flat_rows, flat_rows, (((0,), (0,)), ((), ())), preferred_element_type=jnp.float32
    )
    gram_sum = lax.psum(partial_value, ("samp", "sub"))
    own_center = lax.dynamic_slice_in_dim(centers, owner, 1, 0)
    own_count = lax.dynamic_slice_in_dim(counts, owner, 1, 0)
    covariance = gram_sum / own_count[0] - own_center.T * own_center
    subspace = refine(old_bases[0].astype(jnp.float32), covariance)
    row_mask = jnp.repeat(pattern.astype(jnp.float32), TILE, axis=1)
    errors = cluster_errors(
        scaled,
        row_mask,
        centers,
        lax.all_gather(subspace.astype(jnp.bfloat16)[None], "rows", axis=0, tiled=True),
    )
    return (errors, own_center, subspace[None])


def solution(mesh):
    return jax.shard_map(
        shards,
        mesh=mesh,
        in_specs=(
            P(("groups", "rows", "samp", "sub"), None),
            P("groups"),
            P(("groups", "rows", "samp", "sub"), None),
            P(None, ("groups", "rows", "samp", "sub")),
            P(("groups", "rows"), None, None),
        ),
        out_specs=(
            P(None, ("groups", "rows", "samp", "sub")),
            P(("groups", "rows"), None),
            P(("groups", "rows"), None, None),
        ),
        check_vma=False,
    )
```

profile of v0, /device:TPU:0, one launch (start us, length us, event | category | flops | bytes accessed | tf_op | source)
XLA Modules:
  0.0 230.5 jit_solution(5135596101437912857)
XLA Ops:
  7.2 0.0 copy-start
  7.2 0.7 fusion.19
  7.9 1.1 reduce-window.6
  9.1 0.2 slice_reduce_fusion
  9.3 0.2 reduce-window.9
  9.5 0.1 add_bitcast_fusion
  9.6 0.8 fusion.17
  10.4 0.7 compare_select_fusion
  11.1 20.9 %scatter_custom_fusion = bf16[8192,256]{1,0:T(8,128)(2,1)} fusion(s32[4096]{0:T(1024)S(1)} %bitcast.113, bf16[]{:T(256)} %constant.66.clone.1, bf16[4096,256]{1,0:T(8,128)(2,1)} %param.10, f32[256]{0:T(256)} %param.11), kind=kCustom, calls=%fused_computation.19 | custom fusion | flops 3145728 | bytes 6292482 | tf_op jit(solution)/shard_map/scatter | solution.py:17
  32.0 0.0 copy-start.3
  32.0 0.0 copy-start.1
  32.0 0.0 copy-start.2
  32.1 6.4 %all-to-all-start = ((bf16[4,2048,256]{2,1,0:T(8,128)(2,1)}), bf16[4,2048,256]{2,1,0:T(8,128)(2,1)}, u32[]{:S(2)}, u32[]{:S(2)}) async-start(bf16[4,2048,256]{2,1,0:T(8,128)(2,1)} %bitcast.102), calls=%async_computation | async-start | bytes 8388608 | tf_op jit(solution)/shard_map/all_to_all | solution.py:68
  38.5 0.0 all-reduce.3.cloned.1.call-start
  38.5 0.0 copy-done.3
  38.5 0.0 copy-done.1
  38.5 0.1 convert_reduce_fusion
  38.7 0.0 copy-done.2
  38.7 2.0 multiply_convert_fusion
  40.7 0.4 fusion.18
  41.1 102.7 %all-reduce = (f32[4,256]{1,0:T(4,128)S(1)}, f32[4]{0:T(128)S(1)}) all-reduce(f32[4,256]{1,0:T(4,128)S(1)} %fusion.18, f32[4]{0:T(128)S(1)} %convert_reduce_fusion), channel_id=1, replica_groups=mesh['groups'=2,'rows'=4,'samp'=2,'sub'=2] {'rows','samp','sub'}, use_global_device_ids=true, to_apply=%region_7.8 | all-reduce | flops 1028 | bytes 8224 | tf_op jit(solution)/shard_map/psum | solution.py:65
  143.8 0.1 broadcast_bitcast_fusion
  143.9 0.0 all-to-all-done
  143.9 5.4 %convolution_bitcast_fusion = f32[256,256]{1,0:T(8,128)} fusion(bf16[4,2048,256]{2,1,0:T(8,128)(2,1)} %all-to-all-done), kind=kOutput, calls=%fused_computation.21 | convolution fusion | flops 1073741824 | bytes 4456448 | tf_op jit(solution)/shard_map/dot_general | solution.py:70
  149.3 0.0 all-reduce.3.cloned.1.call-update
  149.4 0.2 multiply_reduce_fusion.1
  149.6 0.6 dynamic_slice.10
  150.2 0.0 copy-start.4
  150.2 36.1 %all-reduce.3.cloned.1.call-done = f32[256,256]{1,0:T(8,128)} async-done(((f32[256,256]{1,0:T(8,128)}), f32[256,256]{1,0:T(8,128)}) %all-reduce.3.cloned.1.call-update) | async-done | bytes 262160 | tf_op jit(solution)/shard_map/psum | solution.py:73
  186.3 0.0 copy-done
  186.3 1.9 fusion.30
  188.2 0.2 fusion.38
  188.4 0.1 copy.15
  188.4 2.9 %cholesky.44 = f32[32,32]{1,0:T(8,128)S(1)} custom-call(f32[32,32]{1,0:T(8,128)S(1)} %fusion.29), custom_call_target="Cholesky" | custom-call | tf_op jit(solution)/shard_map/jit(cholesky)/cholesky | solution.py:25
  191.4 0.7 compare_reduce_fusion.1
  192.1 0.6 fusion.23
  192.7 2.4 %custom-call.6 = f32[1,32,32]{1,2,0:T(8,128)S(1)} custom-call(f32[1,32,32]{2,1,0:T(8,128)S(1)} %fusion.23), custom_call_target="InvertDiagBlocksLowerTriangular" | custom-call | tf_op jit(solution)/shard_map/jit(_solve_triangular)/triangular_solve | solution.py:26
  195.2 0.2 fusion.20
  195.4 1.9 fusion.34
  197.3 0.2 fusion.39
  197.5 0.1 copy.16
  197.6 2.9 %cholesky.55 = f32[32,32]{1,0:T(8,128)S(1)} custom-call(f32[32,32]{1,0:T(8,128)S(1)} %fusion.27), custom_call_target="Cholesky" | custom-call | tf_op jit(solution)/shard_map/jit(cholesky)/cholesky | solution.py:25
  200.5 0.6 compare_reduce_fusion
  201.2 0.7 fusion.24
  201.9 2.4 %custom-call.7 = f32[1,32,32]{1,2,0:T(8,128)S(1)} custom-call(f32[1,32,32]{2,1,0:T(8,128)S(1)} %fusion.24), custom_call_target="InvertDiagBlocksLowerTriangular" | custom-call | tf_op jit(solution)/shard_map/jit(_solve_triangular)/triangular_solve | solution.py:26
  204.3 0.9 fusion.37
  205.2 13.2 %all-gather = bf16[128,256]{1,0:T(8,128)(2,1)S(1)} all-gather(bf16[32,256]{1,0:T(8,128)(2,1)S(1)} %get-tuple-element.61), channel_id=2, replica_groups=mesh['groups'=2,'rows'=4,'samp'=2,'sub'=2] {'rows'}, dimensions={0}, use_global_device_ids=true | all-gather | bytes 81920 | tf_op jit(solution)/shard_map/all_gather | solution.py:83
  218.4 0.2 fusion.35
  218.5 0.0 copy-done.4
  218.5 4.5 %while.10 = (s32[]{:T(128)}, f32[4,1024,4]{1,2,0:T(4,128)S(1)}, bf16[4,1024,256]{2,1,0:T(8,128)(2,1)S(1)}, f32[4,256]{1,0:T(4,128)S(1)}, f32[4]{0:T(128)S(1)}, /...) while((s32[]{:T(128)}, f32[4,1024,4]{1,2,0:T(4,128)S(1)}, ...), condition=%wide.region_14.17_spmd, body=%wide.region_11.16_spmd.sunk | while | flops 80886784 | bytes 1703517 | solution.py:51
  218.6 0.3 fusion.62
  218.9 0.2 multiply_reduce_fusion.3
  219.1 0.5 fusion.63
  219.7 0.3 fusion.62
  220.0 0.2 multiply_reduce_fusion.3
  220.2 0.5 fusion.63
  220.8 0.3 fusion.62
  221.1 0.2 multiply_reduce_fusion.3
  221.3 0.5 fusion.63
  221.9 0.3 fusion.62
  222.2 0.2 multiply_reduce_fusion.3
  222.4 0.5 fusion.63
  223.0 0.7 bitcast_multiply_fusion
  (7 shorter events, 0.1 us)
Async XLA Ops:
  7.2 179.1 %copy-start = (bf16[1,32,256]{2,1,0:T(8,128)(2,1)S(1)}, bf16[1,32,256]{2,1,0:T(8,128)(2,1)}, u32[]{:S(2)}) copy-start(bf16[1,32,256]{2,1,0:T(8,128)(2,1)} %param.14) | copy-start | bytes 49156
  32.0 6.5 %copy-start.3 = (s32[4,32]{1,0:T(4,128)S(1)}, s32[4,32]{1,0:T(4,128)}, u32[]{:S(2)}) copy-start(s32[4,32]{1,0:T(4,128)} %param.13) | copy-start | bytes 1540
  32.0 6.5 %copy-start.1 = (s32[4096,1]{0,1:T(1,128)S(1)}, s32[4096,1]{0,1:T(1,128)}, u32[]{:S(2)}) copy-start(s32[4096,1]{0,1:T(1,128)} %param.12) | copy-start | bytes 49156
  32.0 6.6 %copy-start.2 = (f32[256]{0:T(256)S(1)}, f32[256]{0:T(256)}, u32[]{:S(2)}) copy-start(f32[256]{0:T(256)} %param.11) | copy-start | bytes 3076
  32.1 111.8 %all-to-all-start = ((bf16[4,2048,256]{2,1,0:T(8,128)(2,1)}), bf16[4,2048,256]{2,1,0:T(8,128)(2,1)}, u32[]{:S(2)}, u32[]{:S(2)}) async-start(bf16[4,2048,256]{2,1,0:T(8,128)(2,1)} %bitcast.102), calls=%async_computation | async-start | bytes 8388608 | tf_op jit(solution)/shard_map/all_to_all | solution.py:68
  38.5 147.8 %all-reduce.3.cloned.1.call-start = ((), (), s32[]{:S(2)}) async-start(), calls=%async_computation.1 | async-start | bytes 524288 | tf_op jit(solution)/shard_map/psum | solution.py:73
  150.2 68.4 %copy-start.4 = (f32[1,256]{1,0:T(1,128)}, f32[1,256]{1,0:T(1,128)S(1)}, u32[]{:S(2)}) copy-start(f32[1,256]{1,0:T(1,128)S(1)} %constant_dynamic-slice_fusion) | copy-start | bytes 3076
Sparse Core Ops, SparseCore 0:
  149.5 36.7 all-reduce.2
where the time goes:
time: 231 us
  blocking collectives  116 us (50%)
  other arithmetic  41.9 us (18%)
  waiting for transfers between devices  36.1 us (16%)
  matrix products  14.7 us (6%)
  between operations  14.2 us (6%)
  starting transfers between devices  6.45 us (3%)
    psum x1, blocking collectives, shards(): lax.psum((counts_local, sums_local), ('rows', 'samp', 'sub'))  103 us
    psum x1, waiting for transfers between devices, shards(): gram_sum = lax.psum(partial_value, ('samp', 'sub'))  36.1 us
    scatter x1, other arithmetic, arrange(): jnp.zeros((clusters * capacity, features), scaled.dtype).at[target]  20.9 us
    all_gather x1, blocking collectives, shards(): lax.all_gather(subspace.astype(jnp.bfloat16)[None], 'rows', axis=0, tiled...  13.2 us
    another operation x6, other arithmetic, refine(): factor = jnp.linalg.cholesky(correlation)  7.25 us
    all_to_all x1, starting transfers between devices, shards(): lax.all_to_all(buffer, 'rows', split_axis=0, concat_axis=0, tiled=True)  6.45 us
    another operation x4, other arithmetic, refine(): subspace = jax.scipy.linalg.solve_triangular(factor, mapped, lower=True)  6.15 us
    dot_general x1, matrix products, shards(): lax.dot_general(flat_rows, flat_rows, (((0,), (0,)), ((), ())), preferred...  5.44 us
  transfers between devices with their start and end apart: 2, of which 1 were waited for; matrix products, arithmetic and copies ran while one was open for 1% of the time, Pallas kernels for 0%

commit v1 on v0

v1 whole, which is shorter than its diff:
```python
import functools

import jax
import jax.numpy as jnp
from jax import lax
from jax.experimental import pallas as pl
from jax.experimental.pallas import tpu as pltpu
from jax.sharding import PartitionSpec as P

TILE = 128
STEPS = 2
HALF = 128
F32 = jnp.float32
BF16 = jnp.bfloat16
HIGH = lax.Precision.HIGHEST
NT = (((1,), (1,)), ((), ()))


def round_up(value, unit):
    return -(-value // unit) * unit


def send(src, dst, send_sem, recv_sem, where):
    return pltpu.make_async_remote_copy(
        src_ref=src,
        dst_ref=dst,
        send_sem=send_sem,
        recv_sem=recv_sem,
        device_id=where,
        device_id_type=pl.DeviceIdType.MESH,
    )


def kernel(
    n_rows, n_samp, n_sub,
    points_ref, scale_ref, labels_ref, pattern_ref, old_ref,
    errors_ref, means_ref, bases_ref,
    scaled, flipped, packed, sub_in, half_sum, samp_in, reduced, rows_in, gathered,
    stat, stat_sub_in, stat_half, stat_samp_in, stat_rows, means, square, distance,
    cov, wide, sent,
    s_sub, r_sub, s_samp, r_samp, s_rows, r_rows, s_gat, r_gat,
    s_st_sub, r_st_sub, s_st_samp, r_st_samp, s_st_rows, r_st_rows, s_bas, r_bas,
):
    clusters = n_rows
    rows_total, features = points_ref.shape
    rank = old_ref.shape[0]
    half = 3 * HALF // n_sub
    piece = half // n_samp
    team = n_samp * n_sub
    row = lax.axis_index("rows")
    samp = lax.axis_index("samp")
    sub = lax.axis_index("sub")
    place = sub * n_samp + samp

    def mate(step):
        spot = lax.rem(place + step, team)
        return {"samp": lax.rem(spot, n_samp), "sub": lax.div(spot, n_samp)}

    def other(index, step, size):
        return lax.rem(index + step, size)

    barrier = pltpu.get_barrier_semaphore()
    for step in range(1, team):
        pl.semaphore_signal(barrier, inc=1, device_id=mate(step), device_id_type=pl.DeviceIdType.MESH)
    for step in range(1, n_rows):
        pl.semaphore_signal(
            barrier, inc=1, device_id={"rows": other(row, step, n_rows)},
            device_id_type=pl.DeviceIdType.MESH,
        )

    block = min(512, rows_total)
    for start in range(0, rows_total, block):
        span = slice(start, start + block)
        value = (points_ref[span, :].astype(F32) * scale_ref[...]).astype(BF16)
        scaled[span, :] = value
        turned = value.T
        flipped[:, span] = turned
        full = turned.astype(F32)
        square[:, span] = jnp.sum(full * full, axis=0, keepdims=True)

    padded = means.shape[0]
    labels = labels_ref[...]
    member = (
        lax.broadcasted_iota(jnp.int32, (padded, rows_total), 0) == labels
    ).astype(F32)
    sums = jnp.dot(member.astype(BF16), scaled[...], preferred_element_type=F32)
    counts = jnp.broadcast_to(jnp.sum(member, axis=1, keepdims=True), (padded, features))
    stat[0:clusters, :] = sums[0:clusters]
    stat[clusters : 2 * clusters, :] = counts[0:clusters]

    pl.semaphore_wait(barrier, team - 1 + n_rows - 1)
    sub_peer = {"sub": 1 - sub}

    def sub_copy(c):
        return send(
            packed.at[c, pl.ds(pl.multiple_of((1 - sub) * half, 8), half)],
            sub_in.at[c], s_sub.at[c], r_sub.at[c], sub_peer,
        )

    def samp_copy(c, step):
        peer = other(samp, step, n_samp)
        return send(
            half_sum.at[c, pl.ds(pl.multiple_of(peer * piece, 8), piece)],
            samp_in.at[c, step - 1], s_samp.at[c, step - 1], r_samp.at[c, step - 1],
            {"samp": peer},
        )

    def rows_copy(c, source):
        return send(
            reduced.at[c], rows_in.at[source], s_rows.at[c], r_rows.at[source], {"rows": c}
        )

    stat_sub = send(stat, stat_sub_in, s_st_sub, r_st_sub, sub_peer)
    stat_sub.start()
    stat_samp = [
        send(
            stat_half, stat_samp_in.at[samp], s_st_samp.at[step - 1], r_st_samp.at[step - 1],
            {"samp": other(samp, step, n_samp)},
        )
        for step in range(1, n_samp)
    ]
    stat_row = [
        send(
            stat_rows.at[row], stat_rows.at[row], s_st_rows.at[step - 1], r_st_rows.at[step - 1],
            {"rows": other(row, step, n_rows)},
        )
        for step in range(1, n_rows)
    ]

    def compute(c):
        mask = (labels == c).astype(F32).astype(BF16)
        gram = jnp.dot(flipped[...] * mask, scaled[...], preferred_element_type=F32)
        packed[c, 0:HALF, :] = gram[0:HALF, 0:HALF]
        packed[c, HALF : 2 * HALF, :] = gram[0:HALF, HALF:]
        packed[c, 2 * HALF :, :] = gram[HALF:, HALF:]
        sub_copy(c).start()

    def add_sub(c):
        sub_copy(c).wait_recv()
        half_sum[c] = packed[c, pl.ds(pl.multiple_of(sub * half, 8), half), :] + sub_in[c]
        for step in range(1, n_samp):
            samp_copy(c, step).start()

    def add_samp(c):
        for step in range(1, n_samp):
            samp_copy(c, step).wait_recv()
        total = half_sum[c, pl.ds(pl.multiple_of(samp * piece, 8), piece), :]
        for step in range(1, n_samp):
            total = total + samp_in[c, step - 1]
        reduced[c] = total

        @pl.when(row != c)
        def _():
            rows_copy(c, row).start()

    def stat_stage(stage):
        if stage == 1:
            stat_sub.wait_recv()
            stat_half[...] = stat[...] + stat_sub_in[...]
            for copy in stat_samp:
                copy.start()
            stat_samp_in[samp] = stat_half[...]
        if stage == 2:
            for copy in stat_samp:
                copy.wait_recv()
            total = stat_samp_in[0]
            for index in range(1, n_samp):
                total = total + stat_samp_in[index]
            stat_rows[row] = total
            for copy in stat_row:
                copy.start()
        if stage == 3:
            for copy in stat_row:
                copy.wait_recv()
            total = stat_rows[0]
            for index in range(1, n_rows):
                total = total + stat_rows[index]
            stat[...] = total

    for tick in range(clusters + 2):
        if tick < clusters:
            compute(tick)
        if tick == 1:
            stat_stage(1)
        if 0 <= tick - 1 < clusters:
            add_sub(tick - 1)
        if tick == 2:
            stat_stage(2)
        if 0 <= tick - 2 < clusters:
            add_samp(tick - 2)

    stat_sub.wait_send()
    stat_stage(3)
    centers = stat[0:clusters, :] / stat[clusters : 2 * clusters, :]
    means[...] = jnp.zeros_like(means)
    means[0:clusters, :] = centers
    own = means[pl.ds(row, 1), :]
    own_count = stat[pl.ds(clusters + row, 1), :]
    means_ref[...] = own
    every = means[...]
    top = every.astype(BF16)
    rest = every - top.astype(F32)
    middle = rest.astype(BF16)
    last = (rest - middle.astype(F32)).astype(BF16)
    parts = jnp.concatenate([top, middle, last], axis=0)
    norm = jnp.sum(every * every, axis=1, keepdims=True)
    for start in range(0, rows_total, block):
        span = slice(start, start + block)
        cross = lax.dot_general(parts, scaled[span, :], NT, preferred_element_type=F32)
        cross = cross[0:padded] + (cross[padded : 2 * padded] + cross[2 * padded :])
        distance[:, span] = square[:, span] - 2.0 * cross + norm

    total = reduced[row]
    for step in range(1, n_rows):
        source = other(row, step, n_rows)
        pltpu.make_async_remote_copy(
            src_ref=rows_in.at[source], dst_ref=rows_in.at[source],
            send_sem=s_rows.at[source], recv_sem=r_rows.at[source],
            device_id={"rows": source}, device_id_type=pl.DeviceIdType.MESH,
        ).wait_recv()
        total = total + rows_in[source]
    gathered[place] = total
    gather = [
        send(
            gathered.at[place], gathered.at[place], s_gat.at[step - 1], r_gat.at[step - 1],
            mate(step),
        )
        for step in range(1, team)
    ]
    for copy in gather:
        copy.start()
    wide[...] = jnp.zeros_like(wide)
    for copy in gather:
        copy.wait_recv()
    whole = gathered[...].reshape(3 * HALF, HALF)
    cov[0:HALF, 0:HALF] = whole[0:HALF]
    cov[0:HALF, HALF:] = whole[HALF : 2 * HALF]
    cov[HALF:, 0:HALF] = whole[HALF : 2 * HALF].T
    cov[HALF:, HALF:] = whole[2 * HALF :]

    basis = old_ref[...].astype(F32)
    inverse = 1.0 / own_count
    lane = lax.broadcasted_iota(jnp.int32, (rank, 128), 1)
    line = lax.broadcasted_iota(jnp.int32, (rank, 128), 0)
    for _ in range(STEPS):
        mapped = jnp.dot(basis, cov[...], precision=HIGH, preferred_element_type=F32) * inverse
        mapped = mapped - jnp.sum(basis * own, axis=1, keepdims=True) * own
        wide[rank : 2 * rank, :] = mapped
        table = lax.dot_general(
            mapped, wide[rank : rank + 128, :], NT, precision=HIGH, preferred_element_type=F32
        )
        table = jnp.where(lane == line + rank, 1.0, table)
        for j in range(rank):
            column = jnp.broadcast_to(table[:, j : j + 1], (rank, 128))
            pivot = table[j : j + 1, :] / column[j : j + 1, :]
            table = table - jnp.where(line > j, column, 0.0) * pivot
        diagonal = jnp.sum(jnp.where(lane == line, table, 0.0), axis=1, keepdims=True)
        table = jnp.where(lane < rank, 0.0, table * lax.rsqrt(diagonal))
        basis = jnp.dot(table, wide[0:128, :], precision=HIGH, preferred_element_type=F32)
    bases_ref[...] = basis
    sent[row] = basis.astype(BF16)
    spread = [
        send(
            sent.at[row], sent.at[row], s_bas.at[step - 1], r_bas.at[step - 1],
            {"rows": other(row, step, n_rows)},
        )
        for step in range(1, n_rows)
    ]
    for copy in spread:
        copy.start()
    for copy in spread:
        copy.wait_recv()

    flat = sent[...].reshape(clusters * rank, features)
    shift = [
        jnp.sum(sent[c].astype(F32) * means[c : c + 1, :], axis=1, keepdims=True)
        for c in range(clusters)
    ]
    for start in range(0, rows_total, block):
        span = slice(start, start + block)
        proj = lax.dot_general(flat, scaled[span, :], NT, preferred_element_type=F32)
        for c in range(clusters):
            part = proj[c * rank : (c + 1) * rank] - shift[c]
            value = distance[c : c + 1, span] - jnp.sum(part * part, axis=0, keepdims=True)
            mask = jnp.concatenate(
                [
                    jnp.broadcast_to(pattern_ref[c : c + 1, t : t + 1], (1, TILE))
                    for t in range(start // TILE, (start + block) // TILE)
                ],
                axis=1,
            )
            errors_ref[c : c + 1, span] = mask.astype(F32) * value / features

    for c in range(clusters):
        sub_copy(c).wait_send()
        for step in range(1, n_samp):
            samp_copy(c, step).wait_send()

        @pl.when(row != c)
        def _():
            rows_copy(c, row).wait_send()
    for copy in stat_samp + stat_row + gather + spread:
        copy.wait_send()


def shards(points, inv_scale, labels, pattern, old_bases):
    n_rows = lax.axis_size("rows")
    n_samp = lax.axis_size("samp")
    n_sub = lax.axis_size("sub")
    rows_total, features = points.shape
    rank = old_bases.shape[1]
    clusters = n_rows
    half = 3 * HALF // n_sub
    piece = half // n_samp
    team = n_samp * n_sub
    padded = round_up(clusters, 16)
    dma = pltpu.SemaphoreType.DMA
    vmem = pltpu.VMEM
    specs = pl.BlockSpec(memory_space=pltpu.VMEM)
    errors, centers, subspace = pl.pallas_call(
        functools.partial(kernel, n_rows, n_samp, n_sub),
        out_shape=(
            jax.ShapeDtypeStruct((clusters, rows_total), F32),
            jax.ShapeDtypeStruct((1, features), F32),
            jax.ShapeDtypeStruct((rank, features), F32),
        ),
        in_specs=[specs] * 5,
        out_specs=(specs,) * 3,
        scratch_shapes=[
            vmem((rows_total, features), BF16),
            vmem((features, rows_total), BF16),
            vmem((clusters, 3 * HALF, HALF), F32),
            vmem((clusters, half, HALF), F32),
            vmem((clusters, half, HALF), F32),
            vmem((clusters, n_samp - 1, piece, HALF), F32),
            vmem((clusters, piece, HALF), F32),
            vmem((n_rows, piece, HALF), F32),
            vmem((team, piece, HALF), F32),
            vmem((2 * clusters, features), F32),
            vmem((2 * clusters, features), F32),
            vmem((2 * clusters, features), F32),
            vmem((n_samp, 2 * clusters, features), F32),
            vmem((n_rows, 2 * clusters, features), F32),
            vmem((padded, features), F32),
            vmem((1, rows_total), F32),
            vmem((padded, rows_total), F32),
            vmem((features, features), F32),
            vmem((rank + 128, features), F32),
            vmem((n_rows, rank, features), BF16),
            dma((clusters,)), dma((clusters,)),
            dma((clusters, n_samp - 1)), dma((clusters, n_samp - 1)),
            dma((clusters,)), dma((n_rows,)),
            dma((team - 1,)), dma((team - 1,)),
            dma, dma,
            dma((n_samp - 1,)), dma((n_samp - 1,)),
            dma((n_rows - 1,)), dma((n_rows - 1,)),
            dma((n_rows - 1,)), dma((n_rows - 1,)),
        ],
        compiler_params=pltpu.CompilerParams(
            collective_id=0, has_side_effects=True, vmem_limit_bytes=48 * 1024 * 1024
        ),
    )(
        points,
        inv_scale.reshape(1, features),
        labels.reshape(1, rows_total),
        pattern,
        old_bases[0],
    )
    return (errors, centers, subspace[None])


def solution(mesh):
    return jax.shard_map(
        shards,
        mesh=mesh,
        in_specs=(
            P(("groups", "rows", "samp", "sub"), None),
            P("groups"),
            P(("groups", "rows", "samp", "sub"), None),
            P(None, ("groups", "rows", "samp", "sub")),
            P(("groups", "rows"), None, None),
        ),
        out_specs=(
            P(None, ("groups", "rows", "samp", "sub")),
            P(("groups", "rows"), None),
            P(("groups", "rows"), None, None),
        ),
        check_vma=False,
    )
```

time: 231 us -> 43.7 us (0.19)
  blocking collectives: 116 us -> 0 us
  other arithmetic: 41.9 us -> 0 us
  Pallas kernels: 0 us -> 36.5 us
  waiting for transfers between devices: 36.1 us -> 0 us
  matrix products: 14.7 us -> 0 us
  between operations: 14.2 us -> 0.65 us
  starting transfers between devices: 6.45 us -> 0 us
  local copies, waits for them, and re-layouts: 1.05 us -> 6.19 us
    psum x1 -> x0, blocking collectives: 103 us -> none  [shards(): lax.psum((counts_local, sums_local), ('rows', 'samp', 'sub'))]
    pallas_call x0 -> x1, Pallas kernels: none -> 36.5 us  [shards(): pl.pallas_call(functools.partial(kernel, n_rows, n_samp, n_sub), out_shap...]
    psum x1 -> x0, waiting for transfers between devices: 36.1 us -> none  [shards(): gram_sum = lax.psum(partial_value, ('samp', 'sub'))]
    scatter x1 -> x0, other arithmetic: 20.9 us -> none  [arrange(): jnp.zeros((clusters * capacity, features), scaled.dtype).at[target]]
    another operation x12 -> x0, other arithmetic: 14.8 us -> none  [the longest x6 7.25 us: refine(): factor = jnp.linalg.cholesky(correlation)]
    dot_general x15 -> x0, matrix products: 13.6 us -> none  [the longest x1 5.44 us: shards(): lax.dot_general(flat_rows, flat_rows, (((0,), (0,)), ((), ())), preferred...]
    all_gather x1 -> x0, blocking collectives: 13.2 us -> none  [shards(): lax.all_gather(subspace.astype(jnp.bfloat16)[None], 'rows', axis=0, tiled...]
    all_to_all x1 -> x0, starting transfers between devices: 6.45 us -> none  [shards(): lax.all_to_all(buffer, 'rows', split_axis=0, concat_axis=0, tiled=True)]
  transfers between devices with their start and end apart: 2 -> 0, of which waited for: 1 -> 0; matrix products, arithmetic and copies ran while one was open for 1% -> 0% of each run, Pallas kernels for 0% -> 0%
where the time goes in v1:
time: 43.7 us; the launch traced here: 43.4 us
  Pallas kernels  36.5 us (84%)
  local copies, waits for them, and re-layouts  6.19 us (14%)
  between operations  0.65 us (1%)
    pallas_call x1, Pallas kernels, shards(): pl.pallas_call(functools.partial(kernel, n_rows, n_samp, n_sub), out_shap...  36.5 us
    unnamed x13, local copies, waits for them, and re-layouts  6.19 us

profile of v1, /device:TPU:0, one launch (start us, length us, event | category | flops | bytes accessed | tf_op | source)
XLA Modules:
  0.0 43.4 jit_solution(1720238484864849883)
XLA Ops:
  0.6 0.0 copy-start
  0.6 1.6 %copy-done = bf16[4096,256]{1,0:T(8,128)(2,1)S(1)} copy-done((bf16[4096,256]{1,0:T(8,128)(2,1)S(1)}, bf16[4096,256]{1,0:T(8,128)(2,1)}, u32[]{:S(2)}) %copy-start) | copy-done | bytes 2097176
  2.2 0.0 copy-start.1
  2.2 0.7 %copy-done.1 = s32[4096,1]{0,1:T(1,128)S(1)} copy-done((s32[4096,1]{0,1:T(1,128)S(1)}, s32[4096,1]{0,1:T(1,128)}, u32[]{:S(2)}) %copy-start.1) | copy-done | bytes 16408
  2.9 0.0 copy-start.2
  2.9 0.7 %copy-done.2 = bf16[1,32,256]{2,1,0:T(8,128)(2,1)S(1)} copy-done((bf16[1,32,256]{2,1,0:T(8,128)(2,1)S(1)}, bf16[1,32,256]{2,1,0:T(8,128)(2,1)}, u32[]{:S(2)}) %copy-start.2) | copy-done | bytes 16408
  3.7 0.0 copy-start.3
  3.7 0.7 %copy-done.3 = s32[4,32]{1,0:T(4,128)S(1)} copy-done((s32[4,32]{1,0:T(4,128)S(1)}, s32[4,32]{1,0:T(4,128)}, u32[]{:S(2)}) %copy-start.3) | copy-done | bytes 536
  4.3 0.0 copy-start.4
  4.3 0.7 %copy-done.4 = f32[256]{0:T(256)S(1)} copy-done((f32[256]{0:T(256)S(1)}, f32[256]{0:T(256)}, u32[]{:S(2)}) %copy-start.4) | copy-done | bytes 1048
  5.0 36.5 %shard_map.76 = (f32[4,4096]{1,0:T(4,128)S(1)}, f32[1,256]{1,0:T(1,128)S(1)}, f32[32,256]{1,0:T(8,128)S(1)}) custom-call(bf16[4096,256]{1,0:T(8,128)(2,1)S(1)} %copy-done, f32[1,256]{1,0:T(1,128)S(1)} %bitcast.7, s32[1,4096]{1,0:T(1,128)S(1)} %bitcast.5, s32[4,32]{1,0:T(4,128)S(1)} %copy-done.3, bf16[32,256]{1,0:T(8,128)(2,1)S(1)} %bitcast.6), custom_call_target="tpu_custom_call" | custom-call | tf_op jit(solution)/shard_map/pallas_call | solution.py:320
  41.6 0.6 %copy.11 = f32[4,4096]{1,0:T(4,128)} copy(f32[4,4096]{1,0:T(4,128)S(1)} %get-tuple-element.12) | data formatting | bytes 131072
  42.2 0.6 %copy.12 = f32[1,256]{1,0:T(1,128)} copy(f32[1,256]{1,0:T(1,128)S(1)} %get-tuple-element.13) | data formatting | bytes 2048
  42.8 0.6 %copy.13 = f32[1,32,256]{2,1,0:T(8,128)} copy(f32[1,32,256]{2,1,0:T(8,128)S(1)} %bitcast.4) | data formatting | bytes 65536
Async XLA Ops:
  0.6 1.6 %copy-start = (bf16[4096,256]{1,0:T(8,128)(2,1)S(1)}, bf16[4096,256]{1,0:T(8,128)(2,1)}, u32[]{:S(2)}) copy-start(bf16[4096,256]{1,0:T(8,128)(2,1)} %points_ref.1) | copy-start | bytes 6291460
  2.2 0.7 %copy-start.1 = (s32[4096,1]{0,1:T(1,128)S(1)}, s32[4096,1]{0,1:T(1,128)}, u32[]{:S(2)}) copy-start(s32[4096,1]{0,1:T(1,128)} %param.7) | copy-start | bytes 49156
  2.9 0.7 %copy-start.2 = (bf16[1,32,256]{2,1,0:T(8,128)(2,1)S(1)}, bf16[1,32,256]{2,1,0:T(8,128)(2,1)}, u32[]{:S(2)}) copy-start(bf16[1,32,256]{2,1,0:T(8,128)(2,1)} %param.9) | copy-start | bytes 49156
  3.7 0.7 %copy-start.3 = (s32[4,32]{1,0:T(4,128)S(1)}, s32[4,32]{1,0:T(4,128)}, u32[]{:S(2)}) copy-start(s32[4,32]{1,0:T(4,128)} %pattern_ref.1) | copy-start | bytes 1540
  4.3 0.7 %copy-start.4 = (f32[256]{0:T(256)S(1)}, f32[256]{0:T(256)}, u32[]{:S(2)}) copy-start(f32[256]{0:T(256)} %param.6) | copy-start | bytes 3076

commit v2 on v1

--- a/solution.py
+++ b/solution.py
@@ -10,6 +10,7 @@
 TILE = 128
 STEPS = 2
 HALF = 128
+GROUP = 8
 F32 = jnp.float32
 BF16 = jnp.bfloat16
 HIGH = lax.Precision.HIGHEST
@@ -33,18 +34,19 @@
 
 def kernel(
     n_rows, n_samp, n_sub,
-    points_ref, scale_ref, labels_ref, pattern_ref, old_ref,
+    points_hbm, scale_hbm, labels_hbm, pattern_hbm, old_hbm,
     errors_ref, means_ref, bases_ref,
     scaled, flipped, packed, sub_in, half_sum, samp_in, reduced, rows_in, gathered,
     stat, stat_sub_in, stat_half, stat_samp_in, stat_rows, means, square, distance,
     cov, wide, sent,
+    points_ref, scale_ref, labels_ref, pattern_ref, old_ref, s_in, s_points,
     s_sub, r_sub, s_samp, r_samp, s_rows, r_rows, s_gat, r_gat,
     s_st_sub, r_st_sub, s_st_samp, r_st_samp, s_st_rows, r_st_rows, s_bas, r_bas,
 ):
     clusters = n_rows
     rows_total, features = points_ref.shape
     rank = old_ref.shape[0]
-    half = 3 * HALF // n_sub
+    half = 2 * HALF // n_sub
     piece = half // n_samp
     team = n_samp * n_sub
     row = lax.axis_index("rows")
@@ -69,8 +71,34 @@
         )
 
     block = min(512, rows_total)
+    loads = [
+        pltpu.make_async_copy(
+            points_hbm.at[start : start + block], points_ref.at[start : start + block],
+            s_points.at[start // block],
+        )
+        for start in range(0, rows_total, block)
+    ]
+    extras = [
+        pltpu.make_async_copy(source, target, s_in.at[index])
+        for index, (source, target) in enumerate(
+            (
+                (scale_hbm, scale_ref),
+                (labels_hbm, labels_ref),
+                (pattern_hbm, pattern_ref),
+                (old_hbm, old_ref),
+            )
+        )
+    ]
+    extras[0].start()
+    loads[0].start()
+    extras[1].start()
+    for copy in loads[1:] + extras[2:]:
+        copy.start()
+    extras[0].wait()
+
     for start in range(0, rows_total, block):
         span = slice(start, start + block)
+        loads[start // block].wait()
         value = (points_ref[span, :].astype(F32) * scale_ref[...]).astype(BF16)
         scaled[span, :] = value
         turned = value.T
@@ -78,6 +106,8 @@
         full = turned.astype(F32)
         square[:, span] = jnp.sum(full * full, axis=0, keepdims=True)
 
+    for copy in extras[1:]:
+        copy.wait()
     padded = means.shape[0]
     labels = labels_ref[...]
     member = (
@@ -111,7 +141,6 @@
         )
 
     stat_sub = send(stat, stat_sub_in, s_st_sub, r_st_sub, sub_peer)
-    stat_sub.start()
     stat_samp = [
         send(
             stat_half, stat_samp_in.at[samp], s_st_samp.at[step - 1], r_st_samp.at[step - 1],
@@ -127,13 +156,19 @@
         for step in range(1, n_rows)
     ]
 
+    down = lax.broadcasted_iota(jnp.int32, (HALF, HALF), 0)
+    across = lax.broadcasted_iota(jnp.int32, (HALF, HALF), 1)
+
     def compute(c):
         mask = (labels == c).astype(F32).astype(BF16)
         gram = jnp.dot(flipped[...] * mask, scaled[...], preferred_element_type=F32)
-        packed[c, 0:HALF, :] = gram[0:HALF, 0:HALF]
+        corner, opposite = gram[0:HALF, 0:HALF], gram[HALF:, HALF:]
+        packed[c, 0:HALF, :] = jnp.where(across > down, corner, opposite)
         packed[c, HALF : 2 * HALF, :] = gram[0:HALF, HALF:]
-        packed[c, 2 * HALF :, :] = gram[HALF:, HALF:]
         sub_copy(c).start()
+        stat[clusters + c : clusters + c + 1, 0:HALF] = jnp.sum(
+            jnp.where(across == down, corner, 0.0), axis=0, keepdims=True
+        )
 
     def add_sub(c):
         sub_copy(c).wait_recv()
@@ -177,39 +212,23 @@
                 total = total + stat_rows[index]
             stat[...] = total
 
+    order = sorted(range(clusters), key=lambda c: -abs(2 * c - clusters + 1))
     for tick in range(clusters + 2):
         if tick < clusters:
-            compute(tick)
-        if tick == 1:
+            compute(order[tick])
+        if tick == clusters - 1:
+            stat_sub.start()
+        if 0 <= tick - 1 < clusters:
+            add_sub(order[tick - 1])
+        if tick == clusters:
             stat_stage(1)
-        if 0 <= tick - 1 < clusters:
-            add_sub(tick - 1)
-        if tick == 2:
+        if 0 <= tick - 2 < clusters:
+            add_samp(order[tick - 2])
+        if tick == clusters + 1:
             stat_stage(2)
-        if 0 <= tick - 2 < clusters:
-            add_samp(tick - 2)
-
-    stat_sub.wait_send()
-    stat_stage(3)
-    centers = stat[0:clusters, :] / stat[clusters : 2 * clusters, :]
+
+    wide[...] = jnp.zeros_like(wide)
     means[...] = jnp.zeros_like(means)
-    means[0:clusters, :] = centers
-    own = means[pl.ds(row, 1), :]
-    own_count = stat[pl.ds(clusters + row, 1), :]
-    means_ref[...] = own
-    every = means[...]
-    top = every.astype(BF16)
-    rest = every - top.astype(F32)
-    middle = rest.astype(BF16)
-    last = (rest - middle.astype(F32)).astype(BF16)
-    parts = jnp.concatenate([top, middle, last], axis=0)
-    norm = jnp.sum(every * every, axis=1, keepdims=True)
-    for start in range(0, rows_total, block):
-        span = slice(start, start + block)
-        cross = lax.dot_general(parts, scaled[span, :], NT, preferred_element_type=F32)
-        cross = cross[0:padded] + (cross[padded : 2 * padded] + cross[2 * padded :])
-        distance[:, span] = square[:, span] - 2.0 * cross + norm
-
     total = reduced[row]
     for step in range(1, n_rows):
         source = other(row, step, n_rows)
@@ -229,17 +248,42 @@
     ]
     for copy in gather:
         copy.start()
-    wide[...] = jnp.zeros_like(wide)
+
+    stat_sub.wait_send()
+    stat_stage(3)
+    centers = stat[0:clusters, :] / stat[clusters : 2 * clusters, features - 1 :]
+    means[0:clusters, :] = centers
+    own = means[pl.ds(row, 1), :]
+    own_line = stat[pl.ds(clusters + row, 1), :]
+    own_count = own_line[:, HALF:]
+    means_ref[...] = own
+    every = means[...]
+    top = every.astype(BF16)
+    rest = every - top.astype(F32)
+    middle = rest.astype(BF16)
+    last = (rest - middle.astype(F32)).astype(BF16)
+    parts = jnp.concatenate([top, middle, last], axis=0)
+    norm = jnp.sum(every * every, axis=1, keepdims=True)
+    for start in range(0, rows_total, block):
+        span = slice(start, start + block)
+        cross = lax.dot_general(parts, scaled[span, :], NT, preferred_element_type=F32)
+        cross = cross[0:padded] + (cross[padded : 2 * padded] + cross[2 * padded :])
+        distance[:, span] = square[:, span] - 2.0 * cross + norm
+
     for copy in gather:
         copy.wait_recv()
-    whole = gathered[...].reshape(3 * HALF, HALF)
-    cov[0:HALF, 0:HALF] = whole[0:HALF]
-    cov[0:HALF, HALF:] = whole[HALF : 2 * HALF]
-    cov[HALF:, 0:HALF] = whole[HALF : 2 * HALF].T
-    cov[HALF:, HALF:] = whole[2 * HALF :]
+    whole = gathered[...].reshape(2 * HALF, HALF)
+    shared, side = whole[0:HALF], whole[HALF:]
+    turned = shared.T
+    diagonal = own_line[:, 0:HALF]
+    corner = jnp.where(across > down, shared, turned)
+    cov[0:HALF, 0:HALF] = jnp.where(across == down, diagonal, corner)
+    cov[0:HALF, HALF:] = side
+    cov[HALF:, 0:HALF] = side.T
+    cov[HALF:, HALF:] = jnp.where(across > down, turned, shared)
 
     basis = old_ref[...].astype(F32)
-    inverse = 1.0 / own_count
+    inverse = 1.0 / jnp.concatenate([own_count, own_count], axis=1)
     lane = lax.broadcasted_iota(jnp.int32, (rank, 128), 1)
     line = lax.broadcasted_iota(jnp.int32, (rank, 128), 0)
     for _ in range(STEPS):
@@ -250,10 +294,18 @@
             mapped, wide[rank : rank + 128, :], NT, precision=HIGH, preferred_element_type=F32
         )
         table = jnp.where(lane == line + rank, 1.0, table)
-        for j in range(rank):
-            column = jnp.broadcast_to(table[:, j : j + 1], (rank, 128))
-            pivot = table[j : j + 1, :] / column[j : j + 1, :]
-            table = table - jnp.where(line > j, column, 0.0) * pivot
+        for base in range(0, rank, GROUP):
+            columns = [
+                jnp.broadcast_to(table[:, base + i : base + i + 1], (rank, 128))
+                for i in range(GROUP)
+            ]
+            for i in range(GROUP):
+                j = base + i
+                inverse_pivot = 1.0 / columns[i][j : j + 1, :]
+                factor = jnp.where(line > j, columns[i], 0.0)
+                table = table - factor * (table[j : j + 1, :] * inverse_pivot)
+                for k in range(i + 1, GROUP):
+                    columns[k] = columns[k] - factor * (columns[k][j : j + 1, :] * inverse_pivot)
         diagonal = jnp.sum(jnp.where(lane == line, table, 0.0), axis=1, keepdims=True)
         table = jnp.where(lane < rank, 0.0, table * lax.rsqrt(diagonal))
         basis = jnp.dot(table, wide[0:128, :], precision=HIGH, preferred_element_type=F32)
@@ -266,7 +318,7 @@
         )
         for step in range(1, n_rows)
     ]
-    for copy in spread:
+    for copy in reversed(spread):
         copy.start()
     for copy in spread:
         copy.wait_recv()
@@ -303,6 +355,26 @@
         copy.wait_send()
 
 
+def hand_over(n, *refs):
+    sources, targets, sems = refs[:n], refs[n : 2 * n], refs[2 * n]
+    copies = [pltpu.make_async_copy(sources[i], targets[i], sems.at[i]) for i in range(n)]
+    for copy in copies:
+        copy.start()
+    for copy in copies:
+        copy.wait()
+
+
+def deliver(*arrays):
+    n = len(arrays)
+    return pl.pallas_call(
+        functools.partial(hand_over, n),
+        out_shape=tuple(jax.ShapeDtypeStruct(a.shape, a.dtype) for a in arrays),
+        in_specs=[pl.BlockSpec(memory_space=pltpu.VMEM)] * n,
+        out_specs=(pl.BlockSpec(memory_space=pltpu.HBM),) * n,
+        scratch_shapes=[pltpu.SemaphoreType.DMA((n,))],
+    )(*arrays)
+
+
 def shards(points, inv_scale, labels, pattern, old_bases):
     n_rows = lax.axis_size("rows")
     n_samp = lax.axis_size("samp")
@@ -310,7 +382,7 @@
     rows_total, features = points.shape
     rank = old_bases.shape[1]
     clusters = n_rows
-    half = 3 * HALF // n_sub
+    half = 2 * HALF // n_sub
     piece = half // n_samp
     team = n_samp * n_sub
     padded = round_up(clusters, 16)
@@ -324,12 +396,12 @@
             jax.ShapeDtypeStruct((1, features), F32),
             jax.ShapeDtypeStruct((rank, features), F32),
         ),
-        in_specs=[specs] * 5,
+        in_specs=[pl.BlockSpec(memory_space=pl.ANY)] * 5,
         out_specs=(specs,) * 3,
         scratch_shapes=[
             vmem((rows_total, features), BF16),
             vmem((features, rows_total), BF16),
-            vmem((clusters, 3 * HALF, HALF), F32),
+            vmem((clusters, 2 * HALF, HALF), F32),
             vmem((clusters, half, HALF), F32),
             vmem((clusters, half, HALF), F32),
             vmem((clusters, n_samp - 1, piece, HALF), F32),
@@ -347,6 +419,12 @@
             vmem((features, features), F32),
             vmem((rank + 128, features), F32),
             vmem((n_rows, rank, features), BF16),
+            vmem((rows_total, features), BF16),
+            vmem((1, features), F32),
+            vmem((1, rows_total), jnp.int32),
+            vmem(pattern.shape, jnp.int32),
+            vmem((rank, features), BF16),
+            dma((4,)), dma((rows_total // min(512, rows_total),)),
             dma((clusters,)), dma((clusters,)),
             dma((clusters, n_samp - 1)), dma((clusters, n_samp - 1)),
             dma((clusters,)), dma((n_rows,)),
@@ -357,7 +435,7 @@
             dma((n_rows - 1,)), dma((n_rows - 1,)),
         ],
         compiler_params=pltpu.CompilerParams(
-            collective_id=0, has_side_effects=True, vmem_limit_bytes=48 * 1024 * 1024
+            collective_id=0, has_side_effects=True, vmem_limit_bytes=64 * 1024 * 1024 - 160 * 1024
         ),
     )(
         points,
@@ -366,7 +444,7 @@
         pattern,
         old_bases[0],
     )
-    return (errors, centers, subspace[None])
+    return deliver(errors, centers, subspace[None])
 
 
 def solution(mesh):

time: 43.7 us -> 33.8 us (0.77)
  local copies, waits for them, and re-layouts: 6.19 us -> 0 us
  Pallas kernels: 36.5 us -> 33 us
    unnamed x13 -> x0, local copies, waits for them, and re-layouts: 6.19 us -> none
    pallas_call x1, Pallas kernels: 36.5 us -> 31.5 us  [shards(): pl.pallas_call(functools.partial(kernel, n_rows, n_samp, n_sub), out_shap...]
    pallas_call x0 -> x1, Pallas kernels: none -> 1.51 us  [deliver(): pl.pallas_call(functools.partial(hand_over, n), out_shape=tuple((jax.Shap...]
where the time goes in v2:
time: 33.8 us; the launch traced here: 33.6 us
  Pallas kernels  33 us (98%)
  between operations  0.64 us (2%)
    pallas_call x1, Pallas kernels, shards(): pl.pallas_call(functools.partial(kernel, n_rows, n_samp, n_sub), out_shap...  31.5 us
    pallas_call x1, Pallas kernels, deliver(): pl.pallas_call(functools.partial(hand_over, n), out_shape=tuple((jax.Shap...  1.51 us

profile of v2, /device:TPU:0, one launch (start us, length us, event | category | flops | bytes accessed | tf_op | source)
XLA Modules:
  0.0 33.6 jit_solution(1265709307760035964)
XLA Ops:
  0.6 31.5 %shard_map.76 = (f32[4,4096]{1,0:T(4,128)}, f32[1,256]{1,0:T(1,128)}, f32[32,256]{1,0:T(8,128)}) custom-call(bf16[4096,256]{1,0:T(8,128)(2,1)} %points_hbm.1, f32[1,256]{1,0:T(1,128)} %bitcast.7, s32[1,4096]{1,0:T(1,128)} %bitcast.5, s32[4,32]{1,0:T(4,128)} %pattern_hbm.1, bf16[32,256]{1,0:T(8,128)(2,1)} %bitcast.6), custom_call_target="tpu_custom_call" | custom-call | tf_op jit(solution)/shard_map/pallas_call | solution.py:392
  32.1 1.5 %shard_map.77 = (f32[4,4096]{1,0:T(4,128)}, f32[1,256]{1,0:T(1,128)}, f32[1,32,256]{2,1,0:T(8,128)}) custom-call(f32[4,4096]{1,0:T(4,128)} %get-tuple-element.6.refs_0_, f32[1,256]{1,0:T(1,128)} %get-tuple-element.7.refs_1_, f32[1,32,256]{2,1,0:T(8,128)} %bitcast.4), custom_call_target="tpu_custom_call" | custom-call | tf_op jit(solution)/shard_map/pallas_call | solution.py:369

commit v3 on v2

--- a/solution.py
+++ b/solution.py
@@ -10,7 +10,7 @@
 TILE = 128
 STEPS = 2
 HALF = 128
-GROUP = 8
+GROUP = 16
 F32 = jnp.float32
 BF16 = jnp.bfloat16
 HIGH = lax.Precision.HIGHEST
@@ -35,11 +35,12 @@
 def kernel(
     n_rows, n_samp, n_sub,
     points_hbm, scale_hbm, labels_hbm, pattern_hbm, old_hbm,
-    errors_ref, means_ref, bases_ref,
+    errors_hbm, means_hbm, bases_hbm,
     scaled, flipped, packed, sub_in, half_sum, samp_in, reduced, rows_in, gathered,
     stat, stat_sub_in, stat_half, stat_samp_in, stat_rows, means, square, distance,
     cov, wide, sent,
     points_ref, scale_ref, labels_ref, pattern_ref, old_ref, s_in, s_points,
+    errors_ref, means_ref, bases_ref, s_out,
     s_sub, r_sub, s_samp, r_samp, s_rows, r_rows, s_gat, r_gat,
     s_st_sub, r_st_sub, s_st_samp, r_st_samp, s_st_rows, r_st_rows, s_bas, r_bas,
 ):
@@ -70,7 +71,7 @@
             device_id_type=pl.DeviceIdType.MESH,
         )
 
-    block = min(512, rows_total)
+    block = min(1024, rows_total)
     loads = [
         pltpu.make_async_copy(
             points_hbm.at[start : start + block], points_ref.at[start : start + block],
@@ -320,6 +321,12 @@
     ]
     for copy in reversed(spread):
         copy.start()
+    stores = [
+        pltpu.make_async_copy(means_ref, means_hbm, s_out.at[0]),
+        pltpu.make_async_copy(bases_ref, bases_hbm, s_out.at[1]),
+    ]
+    for copy in stores:
+        copy.start()
     for copy in spread:
         copy.wait_recv()
 
@@ -342,6 +349,12 @@
                 axis=1,
             )
             errors_ref[c : c + 1, span] = mask.astype(F32) * value / features
+        stores.append(
+            pltpu.make_async_copy(
+                errors_ref.at[:, span], errors_hbm.at[:, span], s_out.at[2 + start // block]
+            )
+        )
+        stores[-1].start()
 
     for c in range(clusters):
         sub_copy(c).wait_send()
@@ -353,6 +366,8 @@
             rows_copy(c, row).wait_send()
     for copy in stat_samp + stat_row + gather + spread:
         copy.wait_send()
+    for copy in stores:
+        copy.wait()
 
 
 def hand_over(n, *refs):
@@ -388,7 +403,6 @@
     padded = round_up(clusters, 16)
     dma = pltpu.SemaphoreType.DMA
     vmem = pltpu.VMEM
-    specs = pl.BlockSpec(memory_space=pltpu.VMEM)
     errors, centers, subspace = pl.pallas_call(
         functools.partial(kernel, n_rows, n_samp, n_sub),
         out_shape=(
@@ -397,7 +411,7 @@
             jax.ShapeDtypeStruct((rank, features), F32),
         ),
         in_specs=[pl.BlockSpec(memory_space=pl.ANY)] * 5,
-        out_specs=(specs,) * 3,
+        out_specs=(pl.BlockSpec(memory_space=pl.ANY),) * 3,
         scratch_shapes=[
             vmem((rows_total, features), BF16),
             vmem((features, rows_total), BF16),
@@ -424,7 +438,11 @@
             vmem((1, rows_total), jnp.int32),
             vmem(pattern.shape, jnp.int32),
             vmem((rank, features), BF16),
-            dma((4,)), dma((rows_total // min(512, rows_total),)),
+            dma((4,)), dma((rows_total // min(1024, rows_total),)),
+            vmem((clusters, rows_total), F32),
+            vmem((1, features), F32),
+            vmem((rank, features), F32),
+            dma((2 + rows_total // min(1024, rows_total),)),
             dma((clusters,)), dma((clusters,)),
             dma((clusters, n_samp - 1)), dma((clusters, n_samp - 1)),
             dma((clusters,)), dma((n_rows,)),

time: 33.8 us -> 33.3 us (0.985)
  Pallas kernels: 33 us -> 32.5 us
    pallas_call x1, Pallas kernels: 31.5 us -> 31 us  [shards(): pl.pallas_call(functools.partial(kernel, n_rows, n_samp, n_sub), out_shap...]
where the time goes in v3:
time: 33.3 us; the launch traced here: 33.2 us
  Pallas kernels  32.5 us (98%)
  between operations  0.64 us (2%)
    pallas_call x1, Pallas kernels, shards(): pl.pallas_call(functools.partial(kernel, n_rows, n_samp, n_sub), out_shap...  31 us
    pallas_call x1, Pallas kernels, deliver(): pl.pallas_call(functools.partial(hand_over, n), out_shape=tuple((jax.Shap...  1.51 us

profile of v3, /device:TPU:0, one launch (start us, length us, event | category | flops | bytes accessed | tf_op | source)
XLA Modules:
  0.0 33.2 jit_solution(12742439532794037714)
XLA Ops:
  0.6 31.0 %shard_map.76 = (f32[4,4096]{1,0:T(4,128)}, f32[1,256]{1,0:T(1,128)}, f32[32,256]{1,0:T(8,128)}) custom-call(bf16[4096,256]{1,0:T(8,128)(2,1)} %points_hbm.1, f32[1,256]{1,0:T(1,128)} %bitcast.7, s32[1,4096]{1,0:T(1,128)} %bitcast.5, s32[4,32]{1,0:T(4,128)} %pattern_hbm.1, bf16[32,256]{1,0:T(8,128)(2,1)} %bitcast.6), custom_call_target="tpu_custom_call" | custom-call | tf_op jit(solution)/shard_map/pallas_call | solution.py:406
  31.6 1.5 %shard_map.77 = (f32[4,4096]{1,0:T(4,128)}, f32[1,256]{1,0:T(1,128)}, f32[1,32,256]{2,1,0:T(8,128)}) custom-call(f32[4,4096]{1,0:T(4,128)} %get-tuple-element.6.refs_0_, f32[1,256]{1,0:T(1,128)} %get-tuple-element.7.refs_1_, f32[1,32,256]{2,1,0:T(8,128)} %bitcast.4), custom_call_target="tpu_custom_call" | custom-call | tf_op jit(solution)/shard_map/pallas_call | solution.py:384
